TPU v7x, 32 devices: a whole 2x2x4 slice. The times are simulated.
32 devices in a mesh: season: 4 (over y, x), strip: 8 (over z, core).
Axes of the slice: x: 2, y: 2, z: 4, core: 2. Of those that a mesh axis runs over, the one named last changes fastest.
Arguments:
- noise: float32 [32, 128, 1280], P('season', 'strip'), parts along dimension 0, may hold values from -6 to 6
- kern_row: float32 [31], replicated, may hold values from 0.05 to 0.3
- kern_col: float32 [31], replicated, may hold values from 0.05 to 0.3
- base_yield: float32 [16, 128, 1280], P(None, 'strip'), may hold values from 1 to 4
- sensitivity: float32 [16], replicated, may hold values from 0.1 to 0.5
- crop_mask: int32 [16, 128, 1280], P(None, 'strip'), may hold values 0 or 1
- cell_area: float32 [128, 1280], P('strip'), may hold values from 0.2 to 1
- cell_unit: int32 [128, 1280], P('strip'), may hold values from 0 to 815, as said below
- guarantee: float32 [16], replicated, may hold values from 1.5 to 3
- insured: float32 [16], replicated, may hold values from 0.5 to 2
Outputs:
- payout: float32 [32, 128, 1280], P('season', 'strip'), parts along dimension 0
- unit_yield: float32 [32, 16, 816], P('season', None, 'strip'), parts along dimension 0
There are 4 independent parts, one for each index of `season`. A program takes and returns all parts, laid end to end along the dimension named above; an argument that names none is the same for every part. Nothing has to cross between parts.
Inputs may be any that keep to these rules, and one draw needn't show every extreme that they name: `cell_unit`: a cell in grid row r belongs to a unit from 102 * (r // 16 - 1) to 102 * (r // 16 + 2) - 1.
All inputs are finite; a program needn't handle non-finite values. No bound on the sum of `crop_mask` on one device may be relied on, other than what follows from the above.
Results may differ from a plain program's by a relative error of at most 0.0058.
Values may be sent and summed in bfloat16 or wider, within the bound.
A program may use at most 128 MiB of HBM per device.

v0:
```python
import functools

import jax
import jax.numpy as jnp
from jax import lax
from jax.experimental import pallas as pl
from jax.experimental.pallas import tpu as pltpu
from jax.sharding import PartitionSpec as P

UNIT_DEV = 102
SPAN = 112
WIDE = 256
LOG2E = 1.4426950408889634
MESH = pl.DeviceIdType.MESH
F32 = jnp.float32
BF16 = jnp.bfloat16


def dot(a, b):
    return jnp.dot(a, b, preferred_element_type=F32)


def split(x):
    high = x.astype(BF16)
    return high, (x - high.astype(F32)).astype(BF16)


def kernel(
    n,
    noise_hbm,
    kern_row,
    kern_col,
    base_hbm,
    sens,
    mask_hbm,
    area_hbm,
    unit_hbm,
    guar,
    ins,
    pay_out,
    yield_out,
    noise,
    base,
    mask,
    area,
    unit,
    halo_lo,
    halo_hi,
    row_hi,
    row_lo,
    col_hi,
    col_lo,
    smooth_hi,
    smooth_lo,
    field,
    onehot,
    wins,
    wbase,
    wts,
    value,
    part,
    from_lo,
    from_hi,
    short,
    short_lo,
    short_hi,
    turned,
    window,
    pay,
    local_sem,
    halo_send,
    halo_recv,
    part_send,
    part_recv,
    short_send,
    short_recv,
):
    seasons, rows, cols = noise.shape
    crops = base.shape[0] // rows
    taps = kern_row.shape[0]
    reach = (taps - 1) // 2
    many = seasons * crops
    chunks = cols // WIDE
    cells = rows * WIDE
    me = lax.axis_index("strip")
    has_lo, has_hi = me > 0, me < n - 1

    def copies(source, target, sem):
        copy = pltpu.make_async_copy(source, target, local_sem.at[sem])
        copy.start()
        return copy

    get_unit = copies(unit_hbm, unit, 0)
    get_area = copies(area_hbm, area, 1)
    get_mask = copies(mask_hbm, mask, 2)
    get_base = copies(base_hbm, base, 3)
    get_noise = copies(noise_hbm, noise, 4)

    barrier = pltpu.get_barrier_semaphore()

    def each_side(body):
        @pl.when(has_lo)
        def _():
            body(0, me - 1)

        @pl.when(has_hi)
        def _():
            body(1, me + 1)

    each_side(
        lambda side, peer: pl.semaphore_signal(
            barrier, inc=1, device_id={"strip": peer}, device_id_type=MESH
        )
    )
    inner = jnp.logical_and(has_lo, has_hi)

    @pl.when(inner)
    def _():
        pl.semaphore_wait(barrier, 2)

    @pl.when(jnp.logical_not(inner))
    def _():
        pl.semaphore_wait(barrier, 1)

    def halo(side, peer, k):
        at = pl.ds(pl.multiple_of(k * WIDE, WIDE), WIDE)
        return pltpu.make_async_remote_copy(
            src_ref=noise_hbm.at[:, :, at],
            dst_ref=(halo_hi, halo_lo)[side].at[:, :, at],
            send_sem=halo_send.at[side, k],
            recv_sem=halo_recv.at[1 - side, k],
            device_id={"strip": peer},
            device_id_type=MESH,
        )

    def halo_in(side, peer, k):
        at = pl.ds(pl.multiple_of(k * WIDE, WIDE), WIDE)
        target = (halo_lo, halo_hi)[side].at[:, :, at]
        pltpu.make_async_remote_copy(
            src_ref=target,
            dst_ref=target,
            send_sem=halo_send.at[side, k],
            recv_sem=halo_recv.at[side, k],
            device_id={"strip": peer},
            device_id_type=MESH,
        ).wait_recv()

    for k in range(chunks):
        each_side(lambda side, peer, k=k: halo(side, peer, k).start())

    @pl.when(jnp.logical_not(has_lo))
    def _():
        halo_lo[...] = jnp.zeros_like(halo_lo)

    @pl.when(jnp.logical_not(has_hi))
    def _():
        halo_hi[...] = jnp.zeros_like(halo_hi)

    smooth_hi[...] = jnp.zeros_like(smooth_hi)
    smooth_lo[...] = jnp.zeros_like(smooth_lo)
    part[...] = jnp.zeros_like(part)

    def row_block(b, carry):
        shape = (16, 3 * seasons * rows)
        out = lax.broadcasted_iota(jnp.int32, shape, 0) + b * 16
        src = lax.broadcasted_iota(jnp.int32, shape, 1)
        r, s = out // seasons, out % seasons
        block, s2, i = src // (seasons * rows), (src // rows) % seasons, src % rows
        tap = jnp.where(s == s2, (block - 1) * rows + i - r + reach, -1)
        band = jnp.zeros(shape, F32)
        for t in range(taps):
            band = jnp.where(tap == t, kern_row[t], band)
        at = pl.ds(pl.multiple_of(b * 16, 16), 16)
        row_hi[at, :], row_lo[at, :] = split(band)
        return carry

    lax.fori_loop(0, seasons * rows // 16, row_block, 0)

    def col_block(b, carry):
        shape = (16, WIDE)
        src = lax.broadcasted_iota(jnp.int32, shape, 0) + b * 16 - 128
        tap = src - lax.broadcasted_iota(jnp.int32, shape, 1) + reach
        band = jnp.zeros(shape, F32)
        for t in range(taps):
            band = jnp.where(tap == t, kern_col[t], band)
        at = pl.ds(pl.multiple_of(b * 16, 16), 16)
        col_hi[at, :], col_lo[at, :] = split(band)
        return carry

    lax.fori_loop(0, (WIDE + 256) // 16, col_block, 0)

    get_unit.wait()

    def mark(t, carry):
        k, r = t // rows, t % rows
        at = pl.ds(pl.multiple_of(k * WIDE, WIDE), WIDE)
        to = pl.ds(pl.multiple_of(t * WIDE, WIDE), WIDE)
        local = unit[pl.ds(r, 1), at] - (me - 1) * UNIT_DEV
        local = jnp.broadcast_to(local, (16, WIDE)).astype(F32)
        count = lax.broadcasted_iota(jnp.int32, (16, WIDE), 0).astype(F32)
        for b in range(3):
            mine = local - b * UNIT_DEV - count
            mine = mine.astype(BF16)
            for j in range(SPAN // 16):
                hit = jnp.where(mine == BF16(16 * j), BF16(1), BF16(0))
                onehot[b * SPAN + 16 * j : b * SPAN + 16 * j + 16, to] = hit
        return carry

    lax.fori_loop(0, rows * chunks, mark, 0)

    get_area.wait()
    get_mask.wait()
    get_base.wait()

    def weigh(c, carry):
        at = pl.ds(pl.multiple_of(c * rows, rows), rows)
        weight = mask[at, :].astype(F32) * area[...]
        weight = weight.astype(BF16).astype(F32)
        for q in range(cols // 128):
            wts[q, at, :] = weight[:, q * 128 : q * 128 + 128]
        wins[at, :] = weight * ins[c]
        wbase[at, :] = weight * base[at, :]
        return carry

    lax.fori_loop(0, crops, weigh, 0)
    get_noise.wait()

    def step(k, carry):
        @pl.when(k < chunks)
        def _():
            each_side(lambda side, peer: halo_in(side, peer, k))

            at = pl.ds(pl.multiple_of(k * WIDE, WIDE), WIDE)
            total = jnp.zeros((seasons * rows, WIDE), F32)
            for b, source in enumerate((halo_lo, noise, halo_hi)):
                high, low = split(source[:, :, at].reshape(seasons * rows, WIDE))
                lanes = slice(b * seasons * rows, (b + 1) * seasons * rows)
                total += dot(row_hi[:, lanes], high)
                total += dot(row_hi[:, lanes], low)
                total += dot(row_lo[:, lanes], high)
            to = pl.ds(pl.multiple_of(128 + k * WIDE, 128), WIDE)
            smooth_hi[:, to], smooth_lo[:, to] = split(total)

        @pl.when(k >= 1)
        def _():
            start = (k - 1) * WIDE
            at = pl.ds(pl.multiple_of(start, WIDE), WIDE + 256)
            high, low = smooth_hi[:, at], smooth_lo[:, at]
            field[...] = dot(high, col_hi[...]) + dot(low, col_hi[...]) + dot(high, col_lo[...])
            cols_at = pl.ds(pl.multiple_of(start, WIDE), WIDE)

            def fill(r, carry):
                f = field[pl.ds(pl.multiple_of(r * seasons, seasons), seasons), :] * LOG2E
                to = pl.ds(pl.multiple_of(r * WIDE, WIDE), WIDE)
                for c in range(0, crops, 2):
                    pair = [
                        wbase[pl.ds(d * rows + r, 1), cols_at] * jnp.exp2(f * sens[d])
                        for d in (c, c + 1)
                    ]
                    pair = jnp.concatenate(pair, axis=0).astype(BF16)
                    value[c * seasons : (c + 2) * seasons, to] = pair
                own = [
                    wts[(k - 1) * (WIDE // 128) + q, pl.ds(r, crops, stride=rows), :]
                    for q in range(WIDE // 128)
                ]
                value[many : many + crops, to] = jnp.concatenate(own, axis=1).astype(BF16)
                return carry

            lax.fori_loop(0, rows, fill, 0)
            cells_at = pl.ds(pl.multiple_of((k - 1) * cells, cells), cells)
            part[:, : many + crops] += lax.dot_general(
                onehot[:, cells_at],
                value[...],
                (((1,), (1,)), ((), ())),
                preferred_element_type=F32,
            )

        return carry

    lax.fori_loop(0, chunks + 1, step, 0)

    def exchange(source_of, buffers, send, recv):
        def copy(side, peer):
            return pltpu.make_async_remote_copy(
                src_ref=source_of(side),
                dst_ref=buffers[1 - side],
                send_sem=send.at[side],
                recv_sem=recv.at[1 - side],
                device_id={"strip": peer},
                device_id_type=MESH,
            )

        def arrive(side, peer):
            pltpu.make_async_remote_copy(
                src_ref=buffers[side],
                dst_ref=buffers[side],
                send_sem=send.at[side],
                recv_sem=recv.at[side],
                device_id={"strip": peer},
                device_id_type=MESH,
            ).wait_recv()

        each_side(lambda side, peer: copy(side, peer).start())

        @pl.when(jnp.logical_not(has_lo))
        def _():
            buffers[0][...] = jnp.zeros_like(buffers[0])

        @pl.when(jnp.logical_not(has_hi))
        def _():
            buffers[1][...] = jnp.zeros_like(buffers[1])

        each_side(arrive)
        return lambda: each_side(lambda side, peer: copy(side, peer).wait_send())

    part_done = exchange(
        lambda side: part.at[pl.ds(2 * side * SPAN, SPAN)], (from_lo, from_hi), part_send, part_recv
    )
    total = part[SPAN : 2 * SPAN, :] + from_lo[...] + from_hi[...]
    lane_crop = lax.broadcasted_iota(jnp.int32, (128, many), 1) // seasons
    spread = (lane_crop == lax.broadcasted_iota(jnp.int32, (128, many), 0)).astype(BF16)
    first, rest = split(total[:, many:])
    first_area = dot(first, spread)
    rest1, rest2 = split(total[:, many:] - first.astype(F32))
    denom = jnp.maximum(first_area + dot(rest1, spread) + dot(rest2, spread), 1.0)
    yields = total[:, :many] / denom
    guard = jnp.zeros((1, many), F32)
    for c in range(crops):
        guard = jnp.where(lane_crop[:1] == c, guar[c], guard)
    lack = jnp.maximum(guard - yields, 0.0) / guard
    real = lax.broadcasted_iota(jnp.int32, lack.shape, 0) < UNIT_DEV
    short[...] = jnp.where(real, lack, 0.0).astype(BF16)
    short_done = exchange(lambda side: short, (short_lo, short_hi), short_send, short_recv)

    turned[...] = jnp.concatenate([yields, jnp.zeros((128 - SPAN, many), F32)], axis=0).T
    for s in range(seasons):
        yield_out[s] = turned[pl.ds(s, crops, stride=seasons), :UNIT_DEV]

    for b, source in enumerate((short_lo, short, short_hi)):
        window[b * SPAN : (b + 1) * SPAN, :] = source[...].astype(F32)
    facing = window[...].T.astype(BF16)

    def pays(t, carry):
        k, r = t // rows, t % rows
        at = pl.ds(pl.multiple_of(k * WIDE, WIDE), WIDE)
        cells_at = pl.ds(pl.multiple_of(t * WIDE, WIDE), WIDE)
        lacking = dot(facing, onehot[:, cells_at])
        total = jnp.zeros((seasons, WIDE), F32)
        for c in range(crops):
            total += wins[pl.ds(c * rows + r, 1), at] * lacking[c * seasons : (c + 1) * seasons]
        to = pl.ds(pl.multiple_of(r * seasons, seasons), seasons)
        for q in range(WIDE // 128):
            pay[k * (WIDE // 128) + q, to, :] = total[:, q * 128 : q * 128 + 128]
        return carry

    lax.fori_loop(0, rows * chunks, pays, 0)

    for s in range(seasons):
        for q in range(cols // 128):
            out = pay[q, pl.ds(s, rows, stride=seasons), :]
            pay_out[s, :, q * 128 : q * 128 + 128] = out

    for k in range(chunks):
        each_side(lambda side, peer, k=k: halo(side, peer, k).wait_send())
    part_done()
    short_done()


def on_device(
    noise,
    kern_row,
    kern_col,
    base_yield,
    sensitivity,
    crop_mask,
    cell_area,
    cell_unit,
    guarantee,
    insured,
):
    seasons, rows, cols = noise.shape
    crops = base_yield.shape[0]
    many = seasons * crops
    n = lax.axis_size("strip")
    chunks = cols // WIDE
    hbm = pl.BlockSpec(memory_space=pl.ANY)
    smem = pl.BlockSpec(memory_space=pltpu.SMEM)
    vmem = pl.BlockSpec(memory_space=pltpu.VMEM)
    flat = (crops * rows, cols)
    return pl.pallas_call(
        functools.partial(kernel, n),
        out_shape=(
            jax.ShapeDtypeStruct((seasons, rows, cols), F32),
            jax.ShapeDtypeStruct((seasons, crops, UNIT_DEV), F32),
        ),
        in_specs=[hbm, smem, smem, hbm, smem, hbm, hbm, hbm, smem, smem],
        out_specs=(vmem, vmem),
        scratch_shapes=[
            pltpu.VMEM(noise.shape, F32),
            pltpu.VMEM(flat, F32),
            pltpu.VMEM(flat, jnp.int32),
            pltpu.VMEM((rows, cols), F32),
            pltpu.VMEM((rows, cols), jnp.int32),
            pltpu.VMEM(noise.shape, F32),
            pltpu.VMEM(noise.shape, F32),
            pltpu.VMEM((seasons * rows, 3 * seasons * rows), BF16),
            pltpu.VMEM((seasons * rows, 3 * seasons * rows), BF16),
            pltpu.VMEM((WIDE + 256, WIDE), BF16),
            pltpu.VMEM((WIDE + 256, WIDE), BF16),
            pltpu.VMEM((seasons * rows, cols + 256), BF16),
            pltpu.VMEM((seasons * rows, cols + 256), BF16),
            pltpu.VMEM((seasons * rows, WIDE), F32),
            pltpu.VMEM((3 * SPAN, rows * cols), BF16),
            pltpu.VMEM(flat, F32),
            pltpu.VMEM(flat, F32),
            pltpu.VMEM((cols // 128, crops * rows, 128), F32),
            pltpu.VMEM((many + crops, rows * WIDE), BF16),
            pltpu.VMEM((3 * SPAN, many + 128), F32),
            pltpu.VMEM((SPAN, many + 128), F32),
            pltpu.VMEM((SPAN, many + 128), F32),
            pltpu.VMEM((SPAN, many), BF16),
            pltpu.VMEM((SPAN, many), BF16),
            pltpu.VMEM((SPAN, many), BF16),
            pltpu.VMEM((many, 128), F32),
            pltpu.VMEM((3 * SPAN, many), F32),
            pltpu.VMEM((cols // 128, seasons * rows, 128), F32),
            pltpu.SemaphoreType.DMA((5,)),
            pltpu.SemaphoreType.DMA((2, chunks)),
            pltpu.SemaphoreType.DMA((2, chunks)),
            pltpu.SemaphoreType.DMA((2,)),
            pltpu.SemaphoreType.DMA((2,)),
            pltpu.SemaphoreType.DMA((2,)),
            pltpu.SemaphoreType.DMA((2,)),
        ],
        compiler_params=pltpu.CompilerParams(
            collective_id=0, has_side_effects=True, vmem_limit_bytes=56 * 2**20
        ),
    )(
        noise,
        kern_row,
        kern_col,
        base_yield.reshape(flat),
        sensitivity,
        crop_mask.reshape(flat),
        cell_area,
        cell_unit,
        guarantee,
        insured,
    )


def solution(mesh):
    in_specs = (
        P("season", "strip", None),
        P(),
        P(),
        P(None, "strip", None),
        P(),
        P(None, "strip", None),
        P("strip", None),
        P("strip", None),
        P(),
        P(),
    )
    out_specs = (P("season", "strip", None), P("season", None, "strip"))
    return jax.shard_map(
        on_device, mesh=mesh, in_specs=in_specs, out_specs=out_specs, check_vma=False
    )
```

profile of v0, /device:TPU:1, one launch (start us, length us, event | category | flops | bytes accessed | tf_op | source)
XLA Modules:
  0.0 47.4 jit_solution(11657376936436489684)
XLA Ops:
  0.6 44.1 %shard_map.113 = (f32[8,16,1280]{2,1,0:T(8,128)}, f32[8,16,102]{2,1,0:T(8,128)}) custom-call(f32[8,16,1280]{2,1,0:T(8,128)} %noise_hbm.1, f32[31]{0:T(128)} %kern_row.1, f32[31]{0:T(128)} %kern_col.1, f32[256,1280]{1,0:T(8,128)} %bitcast.2, f32[16]{0:T(128)} %sens.1, s32[256,1280]{1,0:T(8,128)} %bitcast.3, f32[16,1280]{1,0:T(8,128)} %area_hbm.1, ...), custom_call_target="tpu_custom_call" | custom-call | tf_op jit(solution)/shard_map/pallas_call | solution.py:390
  44.7 0.0 copy-start
  44.7 2.0 %copy.14 = f32[8,16,1280]{2,1,0:T(8,128)} copy(f32[8,16,1280]{2,1,0:T(8,128)} %get-tuple-element.4) | data formatting | bytes 1310720
  46.7 0.0 copy-done
  46.7 0.6 %copy.15 = f32[8,16,102]{2,1,0:T(8,128)} copy(f32[8,16,102]{2,1,0:T(8,128)S(1)} %copy-done) | data formatting | bytes 104448
Async XLA Ops:
  44.7 2.0 %copy-start = (f32[8,16,102]{2,1,0:T(8,128)S(1)}, f32[8,16,102]{2,1,0:T(8,128)}, u32[]{:S(2)}) copy-start(f32[8,16,102]{2,1,0:T(8,128)} %get-tuple-element.5) | copy-start | bytes 156676
where the time goes:
time: 47.5 us; the launch traced here: 47.4 us
  Pallas kernels  44.1 us (93%)
  local copies, waits for them, and re-layouts  2.64 us (6%)
  between operations  0.65 us (1%)
    pallas_call x1, Pallas kernels, on_device(): pl.pallas_call(functools.partial(kernel, n), out_shape=(jax.ShapeDtypeStr...  44.1 us
    unnamed x4, local copies, waits for them, and re-layouts  2.64 us

commit v1 on v0

--- a/solution.py
+++ b/solution.py
@@ -8,7 +8,10 @@
 from jax.sharding import PartitionSpec as P
 
 UNIT_DEV = 102
-SPAN = 112
+SPAN = 104
+SHORT = 112
+SLOTS = 320
+GROUP = 4
 WIDE = 256
 LOG2E = 1.4426950408889634
 MESH = pl.DeviceIdType.MESH
@@ -46,10 +49,8 @@
     unit,
     halo_lo,
     halo_hi,
-    row_hi,
-    row_lo,
-    col_hi,
-    col_lo,
+    row_band,
+    col_band,
     smooth_hi,
     smooth_lo,
     field,
@@ -57,16 +58,15 @@
     wins,
     wbase,
     wts,
-    value,
+    value_a,
+    value_b,
     part,
     from_lo,
     from_hi,
     short,
     short_lo,
     short_hi,
-    turned,
     window,
-    pay,
     local_sem,
     halo_send,
     halo_recv,
@@ -81,7 +81,6 @@
     reach = (taps - 1) // 2
     many = seasons * crops
     chunks = cols // WIDE
-    cells = rows * WIDE
     me = lax.axis_index("strip")
     has_lo, has_hi = me > 0, me < n - 1
 
@@ -171,20 +170,23 @@
         for t in range(taps):
             band = jnp.where(tap == t, kern_row[t], band)
         at = pl.ds(pl.multiple_of(b * 16, 16), 16)
-        row_hi[at, :], row_lo[at, :] = split(band)
+        high, low = split(band)
+        row_band[at, :] = jnp.concatenate([high, high, low], axis=1)
         return carry
 
     lax.fori_loop(0, seasons * rows // 16, row_block, 0)
 
-    def col_block(b, carry):
+    def col_block(j, carry):
         shape = (16, WIDE)
-        src = lax.broadcasted_iota(jnp.int32, shape, 0) + b * 16 - 128
+        src = lax.broadcasted_iota(jnp.int32, shape, 0) + j * 16 - 128
         tap = src - lax.broadcasted_iota(jnp.int32, shape, 1) + reach
         band = jnp.zeros(shape, F32)
         for t in range(taps):
             band = jnp.where(tap == t, kern_col[t], band)
-        at = pl.ds(pl.multiple_of(b * 16, 16), 16)
-        col_hi[at, :], col_lo[at, :] = split(band)
+        high, low = split(band)
+        for b, piece in enumerate((high, high, low)):
+            to = pl.ds(pl.multiple_of(b * (WIDE + 256) + j * 16, 16), 16)
+            col_band[to, :] = piece
         return carry
 
     lax.fori_loop(0, (WIDE + 256) // 16, col_block, 0)
@@ -196,14 +198,13 @@
         at = pl.ds(pl.multiple_of(k * WIDE, WIDE), WIDE)
         to = pl.ds(pl.multiple_of(t * WIDE, WIDE), WIDE)
         local = unit[pl.ds(r, 1), at] - (me - 1) * UNIT_DEV
-        local = jnp.broadcast_to(local, (16, WIDE)).astype(F32)
-        count = lax.broadcasted_iota(jnp.int32, (16, WIDE), 0).astype(F32)
-        for b in range(3):
-            mine = local - b * UNIT_DEV - count
-            mine = mine.astype(BF16)
-            for j in range(SPAN // 16):
-                hit = jnp.where(mine == BF16(16 * j), BF16(1), BF16(0))
-                onehot[b * SPAN + 16 * j : b * SPAN + 16 * j + 16, to] = hit
+        past = jnp.where(local >= UNIT_DEV, 1, 0) + jnp.where(local >= 2 * UNIT_DEV, 1, 0)
+        slot = local + past * (SPAN - UNIT_DEV) - SLOTS // 2
+        slot = jnp.broadcast_to(slot, (16, WIDE))
+        slot = (slot - lax.broadcasted_iota(jnp.int32, (16, WIDE), 0)).astype(F32).astype(BF16)
+        for j in range(SLOTS // 16):
+            hit = jnp.where(slot == BF16(16 * j - SLOTS // 2), BF16(1), BF16(0))
+            onehot[16 * j : 16 * j + 16, to] = hit
         return carry
 
     lax.fori_loop(0, rows * chunks, mark, 0)
@@ -225,19 +226,29 @@
     lax.fori_loop(0, crops, weigh, 0)
     get_noise.wait()
 
+    value_b[...] = jnp.zeros_like(value_b)
+
+    def add(value, index):
+        at = pl.ds(pl.multiple_of(index * GROUP * WIDE, GROUP * WIDE), GROUP * WIDE)
+        part[:, : many + crops] += lax.dot_general(
+            onehot[:, at],
+            value[...],
+            (((1,), (1,)), ((), ())),
+            preferred_element_type=F32,
+        )
+
     def step(k, carry):
         @pl.when(k < chunks)
         def _():
             each_side(lambda side, peer: halo_in(side, peer, k))
 
             at = pl.ds(pl.multiple_of(k * WIDE, WIDE), WIDE)
-            total = jnp.zeros((seasons * rows, WIDE), F32)
-            for b, source in enumerate((halo_lo, noise, halo_hi)):
-                high, low = split(source[:, :, at].reshape(seasons * rows, WIDE))
-                lanes = slice(b * seasons * rows, (b + 1) * seasons * rows)
-                total += dot(row_hi[:, lanes], high)
-                total += dot(row_hi[:, lanes], low)
-                total += dot(row_lo[:, lanes], high)
+            parts = [
+                split(source[:, :, at].reshape(seasons * rows, WIDE))
+                for source in (halo_lo, noise, halo_hi)
+            ]
+            highs, lows = [p[0] for p in parts], [p[1] for p in parts]
+            total = dot(row_band[...], jnp.concatenate(highs + lows + highs, axis=0))
             to = pl.ds(pl.multiple_of(128 + k * WIDE, 128), WIDE)
             smooth_hi[:, to], smooth_lo[:, to] = split(total)
 
@@ -246,12 +257,11 @@
             start = (k - 1) * WIDE
             at = pl.ds(pl.multiple_of(start, WIDE), WIDE + 256)
             high, low = smooth_hi[:, at], smooth_lo[:, at]
-            field[...] = dot(high, col_hi[...]) + dot(low, col_hi[...]) + dot(high, col_lo[...])
+            field[...] = dot(jnp.concatenate([high, low, high], axis=1), col_band[...]) * LOG2E
             cols_at = pl.ds(pl.multiple_of(start, WIDE), WIDE)
 
-            def fill(r, carry):
-                f = field[pl.ds(pl.multiple_of(r * seasons, seasons), seasons), :] * LOG2E
-                to = pl.ds(pl.multiple_of(r * WIDE, WIDE), WIDE)
+            def fill(value, r, to):
+                f = field[pl.ds(pl.multiple_of(r * seasons, seasons), seasons), :]
                 for c in range(0, crops, 2):
                     pair = [
                         wbase[pl.ds(d * rows + r, 1), cols_at] * jnp.exp2(f * sens[d])
@@ -264,20 +274,21 @@
                     for q in range(WIDE // 128)
                 ]
                 value[many : many + crops, to] = jnp.concatenate(own, axis=1).astype(BF16)
+
+            def group(i, carry):
+                for half, (before, now) in enumerate(((value_b, value_a), (value_a, value_b))):
+                    first = 2 * i + half
+                    add(before, jnp.maximum((k - 1) * (rows // GROUP) + first - 1, 0))
+                    for j in range(GROUP):
+                        fill(now, first * GROUP + j, slice(j * WIDE, j * WIDE + WIDE))
                 return carry
 
-            lax.fori_loop(0, rows, fill, 0)
-            cells_at = pl.ds(pl.multiple_of((k - 1) * cells, cells), cells)
-            part[:, : many + crops] += lax.dot_general(
-                onehot[:, cells_at],
-                value[...],
-                (((1,), (1,)), ((), ())),
-                preferred_element_type=F32,
-            )
+            lax.fori_loop(0, rows // (2 * GROUP), group, 0)
 
         return carry
 
     lax.fori_loop(0, chunks + 1, step, 0)
+    add(value_b, chunks * (rows // GROUP) - 1)
 
     def exchange(source_of, buffers, send, recv):
         def copy(side, peer):
@@ -329,15 +340,16 @@
         guard = jnp.where(lane_crop[:1] == c, guar[c], guard)
     lack = jnp.maximum(guard - yields, 0.0) / guard
     real = lax.broadcasted_iota(jnp.int32, lack.shape, 0) < UNIT_DEV
-    short[...] = jnp.where(real, lack, 0.0).astype(BF16)
+    lack = jnp.where(real, lack, 0.0)
+    none = jnp.zeros((SHORT - SPAN, many), F32)
+    short[...] = jnp.concatenate([lack, none], axis=0).astype(BF16)
     short_done = exchange(lambda side: short, (short_lo, short_hi), short_send, short_recv)
 
-    turned[...] = jnp.concatenate([yields, jnp.zeros((128 - SPAN, many), F32)], axis=0).T
-    for s in range(seasons):
-        yield_out[s] = turned[pl.ds(s, crops, stride=seasons), :UNIT_DEV]
+    yield_out[...] = jnp.concatenate([yields, jnp.zeros((128 - SPAN, many), F32)], axis=0).T
 
     for b, source in enumerate((short_lo, short, short_hi)):
-        window[b * SPAN : (b + 1) * SPAN, :] = source[...].astype(F32)
+        window[b * SPAN : (b + 1) * SPAN, :] = source[...].astype(F32)[:SPAN]
+    window[3 * SPAN :, :] = jnp.zeros((SLOTS - 3 * SPAN, many), F32)
     facing = window[...].T.astype(BF16)
 
     def pays(t, carry):
@@ -350,20 +362,25 @@
             total += wins[pl.ds(c * rows + r, 1), at] * lacking[c * seasons : (c + 1) * seasons]
         to = pl.ds(pl.multiple_of(r * seasons, seasons), seasons)
         for q in range(WIDE // 128):
-            pay[k * (WIDE // 128) + q, to, :] = total[:, q * 128 : q * 128 + 128]
-        return carry
-
-    lax.fori_loop(0, rows * chunks, pays, 0)
-
-    for s in range(seasons):
-        for q in range(cols // 128):
-            out = pay[q, pl.ds(s, rows, stride=seasons), :]
-            pay_out[s, :, q * 128 : q * 128 + 128] = out
+            pay_out[k * (WIDE // 128) + q, to, :] = total[:, q * 128 : q * 128 + 128]
+        return carry
+
+    lax.fori_loop(0, rows * chunks, pays, 0, unroll=8)
 
     for k in range(chunks):
         each_side(lambda side, peer, k=k: halo(side, peer, k).wait_send())
     part_done()
     short_done()
+
+
+def unravel(pay, yields, pay_out, yield_out):
+    seasons, rows, cols = pay_out.shape
+    crops = yield_out.shape[1]
+    for s in range(seasons):
+        yield_out[s] = yields[pl.ds(s, crops, stride=seasons), :][:, :UNIT_DEV]
+        for q in range(cols // 128):
+            out = pay[q, pl.ds(s, rows, stride=seasons), :]
+            pay_out[s, :, q * 128 : q * 128 + 128] = out
 
 
 def on_device(
@@ -387,11 +404,11 @@
     smem = pl.BlockSpec(memory_space=pltpu.SMEM)
     vmem = pl.BlockSpec(memory_space=pltpu.VMEM)
     flat = (crops * rows, cols)
-    return pl.pallas_call(
+    pay, yields = pl.pallas_call(
         functools.partial(kernel, n),
         out_shape=(
-            jax.ShapeDtypeStruct((seasons, rows, cols), F32),
-            jax.ShapeDtypeStruct((seasons, crops, UNIT_DEV), F32),
+            jax.ShapeDtypeStruct((cols // 128, seasons * rows, 128), F32),
+            jax.ShapeDtypeStruct((many, 128), F32),
         ),
         in_specs=[hbm, smem, smem, hbm, smem, hbm, hbm, hbm, smem, smem],
         out_specs=(vmem, vmem),
@@ -403,27 +420,24 @@
             pltpu.VMEM((rows, cols), jnp.int32),
             pltpu.VMEM(noise.shape, F32),
             pltpu.VMEM(noise.shape, F32),
-            pltpu.VMEM((seasons * rows, 3 * seasons * rows), BF16),
-            pltpu.VMEM((seasons * rows, 3 * seasons * rows), BF16),
-            pltpu.VMEM((WIDE + 256, WIDE), BF16),
-            pltpu.VMEM((WIDE + 256, WIDE), BF16),
+            pltpu.VMEM((seasons * rows, 9 * seasons * rows), BF16),
+            pltpu.VMEM((3 * (WIDE + 256), WIDE), BF16),
             pltpu.VMEM((seasons * rows, cols + 256), BF16),
             pltpu.VMEM((seasons * rows, cols + 256), BF16),
             pltpu.VMEM((seasons * rows, WIDE), F32),
-            pltpu.VMEM((3 * SPAN, rows * cols), BF16),
+            pltpu.VMEM((SLOTS, rows * cols), BF16),
             pltpu.VMEM(flat, F32),
             pltpu.VMEM(flat, F32),
             pltpu.VMEM((cols // 128, crops * rows, 128), F32),
-            pltpu.VMEM((many + crops, rows * WIDE), BF16),
-            pltpu.VMEM((3 * SPAN, many + 128), F32),
+            pltpu.VMEM((many + crops, GROUP * WIDE), BF16),
+            pltpu.VMEM((many + crops, GROUP * WIDE), BF16),
+            pltpu.VMEM((SLOTS, many + 128), F32),
             pltpu.VMEM((SPAN, many + 128), F32),
             pltpu.VMEM((SPAN, many + 128), F32),
-            pltpu.VMEM((SPAN, many), BF16),
-            pltpu.VMEM((SPAN, many), BF16),
-            pltpu.VMEM((SPAN, many), BF16),
-            pltpu.VMEM((many, 128), F32),
-            pltpu.VMEM((3 * SPAN, many), F32),
-            pltpu.VMEM((cols // 128, seasons * rows, 128), F32),
+            pltpu.VMEM((SHORT, many), BF16),
+            pltpu.VMEM((SHORT, many), BF16),
+            pltpu.VMEM((SHORT, many), BF16),
+            pltpu.VMEM((SLOTS, many), F32),
             pltpu.SemaphoreType.DMA((5,)),
             pltpu.SemaphoreType.DMA((2, chunks)),
             pltpu.SemaphoreType.DMA((2, chunks)),
@@ -447,6 +461,15 @@
         guarantee,
         insured,
     )
+    return pl.pallas_call(
+        unravel,
+        out_shape=(
+            jax.ShapeDtypeStruct((seasons, rows, cols), F32),
+            jax.ShapeDtypeStruct((seasons, crops, UNIT_DEV), F32),
+        ),
+        in_specs=[vmem, vmem],
+        out_specs=(vmem, vmem),
+    )(pay, yields)
 
 
 def solution(mesh):

time: 47.5 us -> 33 us (0.69)
  Pallas kernels: 44.1 us -> 32.2 us
  local copies, waits for them, and re-layouts: 2.64 us -> 0 us
    pallas_call x1, Pallas kernels: 44.1 us -> 30.1 us  [on_device(): pl.pallas_call(functools.partial(kernel, n), out_shape=(jax.ShapeDtypeStr...]
    unnamed x4 -> x0, local copies, waits for them, and re-layouts: 2.64 us -> none
    pallas_call x0 -> x1, Pallas kernels: none -> 2.06 us  [on_device(): pl.pallas_call(unravel, out_shape=(jax.ShapeDtypeStruct((seasons, rows, c...]
where the time goes in v1:
time: 33 us; the launch traced here: 32.8 us
  Pallas kernels  32.2 us (98%)
  between operations  0.64 us (2%)
    pallas_call x1, Pallas kernels, on_device(): pl.pallas_call(functools.partial(kernel, n), out_shape=(jax.ShapeDtypeStr...  30.1 us
    pallas_call x1, Pallas kernels, on_device(): pl.pallas_call(unravel, out_shape=(jax.ShapeDtypeStruct((seasons, rows, c...  2.06 us

profile of v1, /device:TPU:1, one launch (start us, length us, event | category | flops | bytes accessed | tf_op | source)
XLA Modules:
  0.0 32.8 jit_solution(6449985729486330610)
XLA Ops:
  0.6 30.1 %shard_map.113 = (f32[10,128,128]{2,1,0:T(8,128)}, f32[128,128]{1,0:T(8,128)}) custom-call(f32[8,16,1280]{2,1,0:T(8,128)} %noise_hbm.1, f32[31]{0:T(128)} %kern_row.1, f32[31]{0:T(128)} %kern_col.1, f32[256,1280]{1,0:T(8,128)} %bitcast.2, f32[16]{0:T(128)} %sens.1, s32[256,1280]{1,0:T(8,128)} %bitcast.3, f32[16,1280]{1,0:T(8,128)} %area_hbm.1, ...), custom_call_target="tpu_custom_call" | custom-call | tf_op jit(solution)/shard_map/pallas_call | solution.py:407
  30.8 2.1 %shard_map.114 = (f32[8,16,1280]{2,1,0:T(8,128)}, f32[8,16,102]{2,1,0:T(8,128)}) custom-call(f32[10,128,128]{2,1,0:T(8,128)} %get-tuple-element.4.pay, f32[128,128]{1,0:T(8,128)} %get-tuple-element.5.yields), custom_call_target="tpu_custom_call" | custom-call | tf_op jit(solution)/shard_map/pallas_call | solution.py:464

commit v2 on v1

--- a/solution.py
+++ b/solution.py
@@ -11,7 +11,7 @@
 SPAN = 104
 SHORT = 112
 SLOTS = 320
-GROUP = 4
+GROUP = 8
 WIDE = 256
 LOG2E = 1.4426950408889634
 MESH = pl.DeviceIdType.MESH
@@ -207,7 +207,7 @@
             onehot[16 * j : 16 * j + 16, to] = hit
         return carry
 
-    lax.fori_loop(0, rows * chunks, mark, 0)
+    lax.fori_loop(0, rows * chunks, mark, 0, unroll=2)
 
     get_area.wait()
     get_mask.wait()
@@ -237,57 +237,61 @@
             preferred_element_type=F32,
         )
 
+    def smooth_rows(k):
+        each_side(lambda side, peer: halo_in(side, peer, k))
+        at = pl.ds(pl.multiple_of(k * WIDE, WIDE), WIDE)
+        parts = [
+            split(source[:, :, at].reshape(seasons * rows, WIDE))
+            for source in (halo_lo, noise, halo_hi)
+        ]
+        highs, lows = [p[0] for p in parts], [p[1] for p in parts]
+        total = dot(row_band[...], jnp.concatenate(highs + lows + highs, axis=0))
+        to = pl.ds(pl.multiple_of(128 + k * WIDE, 128), WIDE)
+        smooth_hi[:, to], smooth_lo[:, to] = split(total)
+
+    def smooth_cols(k):
+        at = pl.ds(pl.multiple_of(k * WIDE, WIDE), WIDE + 256)
+        high, low = smooth_hi[:, at], smooth_lo[:, at]
+        return dot(jnp.concatenate([high, low, high], axis=1), col_band[...]) * LOG2E
+
+    def fill(value, k, r, to):
+        cols_at = pl.ds(pl.multiple_of(k * WIDE, WIDE), WIDE)
+        f = field[r * seasons : (r + 1) * seasons, :]
+        for c in range(0, crops, 2):
+            pair = [
+                wbase[pl.ds(d * rows + r, 1), cols_at] * jnp.exp2(f * sens[d])
+                for d in (c, c + 1)
+            ]
+            pair = jnp.concatenate(pair, axis=0).astype(BF16)
+            value[c * seasons : (c + 2) * seasons, to] = pair
+        own = [
+            wts[k * (WIDE // 128) + q, pl.ds(r, crops, stride=rows), :]
+            for q in range(WIDE // 128)
+        ]
+        value[many : many + crops, to] = jnp.concatenate(own, axis=1).astype(BF16)
+
+    def consume(k):
+        for first in range(rows // GROUP):
+            before, now = ((value_b, value_a), (value_a, value_b))[first % 2]
+            add(before, jnp.maximum(k * (rows // GROUP) + first - 1, 0))
+            for j in range(GROUP):
+                fill(now, k, first * GROUP + j, slice(j * WIDE, j * WIDE + WIDE))
+
     def step(k, carry):
-        @pl.when(k < chunks)
-        def _():
-            each_side(lambda side, peer: halo_in(side, peer, k))
-
-            at = pl.ds(pl.multiple_of(k * WIDE, WIDE), WIDE)
-            parts = [
-                split(source[:, :, at].reshape(seasons * rows, WIDE))
-                for source in (halo_lo, noise, halo_hi)
-            ]
-            highs, lows = [p[0] for p in parts], [p[1] for p in parts]
-            total = dot(row_band[...], jnp.concatenate(highs + lows + highs, axis=0))
-            to = pl.ds(pl.multiple_of(128 + k * WIDE, 128), WIDE)
-            smooth_hi[:, to], smooth_lo[:, to] = split(total)
-
-        @pl.when(k >= 1)
-        def _():
-            start = (k - 1) * WIDE
-            at = pl.ds(pl.multiple_of(start, WIDE), WIDE + 256)
-            high, low = smooth_hi[:, at], smooth_lo[:, at]
-            field[...] = dot(jnp.concatenate([high, low, high], axis=1), col_band[...]) * LOG2E
-            cols_at = pl.ds(pl.multiple_of(start, WIDE), WIDE)
-
-            def fill(value, r, to):
-                f = field[pl.ds(pl.multiple_of(r * seasons, seasons), seasons), :]
-                for c in range(0, crops, 2):
-                    pair = [
-                        wbase[pl.ds(d * rows + r, 1), cols_at] * jnp.exp2(f * sens[d])
-                        for d in (c, c + 1)
-                    ]
-                    pair = jnp.concatenate(pair, axis=0).astype(BF16)
-                    value[c * seasons : (c + 2) * seasons, to] = pair
-                own = [
-                    wts[(k - 1) * (WIDE // 128) + q, pl.ds(r, crops, stride=rows), :]
-                    for q in range(WIDE // 128)
-                ]
-                value[many : many + crops, to] = jnp.concatenate(own, axis=1).astype(BF16)
-
-            def group(i, carry):
-                for half, (before, now) in enumerate(((value_b, value_a), (value_a, value_b))):
-                    first = 2 * i + half
-                    add(before, jnp.maximum((k - 1) * (rows // GROUP) + first - 1, 0))
-                    for j in range(GROUP):
-                        fill(now, first * GROUP + j, slice(j * WIDE, j * WIDE + WIDE))
-                return carry
-
-            lax.fori_loop(0, rows // (2 * GROUP), group, 0)
-
+        smooth_rows(k)
+        following = smooth_cols(k - 1)
+        consume(k - 2)
+        field[...] = following
         return carry
 
-    lax.fori_loop(0, chunks + 1, step, 0)
+    smooth_rows(0)
+    smooth_rows(1)
+    field[...] = smooth_cols(0)
+    lax.fori_loop(2, chunks, step, 0)
+    following = smooth_cols(chunks - 1)
+    consume(chunks - 2)
+    field[...] = following
+    consume(chunks - 1)
     add(value_b, chunks * (rows // GROUP) - 1)
 
     def exchange(source_of, buffers, send, recv):
@@ -365,7 +369,7 @@
             pay_out[k * (WIDE // 128) + q, to, :] = total[:, q * 128 : q * 128 + 128]
         return carry
 
-    lax.fori_loop(0, rows * chunks, pays, 0, unroll=8)
+    lax.fori_loop(0, rows * chunks, pays, 0, unroll=16)
 
     for k in range(chunks):
         each_side(lambda side, peer, k=k: halo(side, peer, k).wait_send())
@@ -467,8 +471,15 @@
             jax.ShapeDtypeStruct((seasons, rows, cols), F32),
             jax.ShapeDtypeStruct((seasons, crops, UNIT_DEV), F32),
         ),
-        in_specs=[vmem, vmem],
-        out_specs=(vmem, vmem),
+        grid=(2,),
+        in_specs=[
+            pl.BlockSpec((cols // 256, seasons * rows, 128), lambda i: (i, 0, 0)),
+            pl.BlockSpec((many, 128), lambda i: (0, 0)),
+        ],
+        out_specs=(
+            pl.BlockSpec((seasons, rows, cols // 2), lambda i: (0, 0, i)),
+            pl.BlockSpec((seasons, crops, UNIT_DEV), lambda i: (0, 0, 0)),
+        ),
     )(pay, yields)
 
 

time: 33 us -> 30.4 us (0.921)
  Pallas kernels: 32.2 us -> 29.6 us
    pallas_call x1, Pallas kernels: 30.1 us -> 27.7 us  [on_device(): pl.pallas_call(functools.partial(kernel, n), out_shape=(jax.ShapeDtypeStr...]
where the time goes in v2:
time: 30.4 us; the launch traced here: 30.3 us
  Pallas kernels  29.6 us (97%)
  between operations  0.64 us (2%)
    pallas_call x1, Pallas kernels, on_device(): pl.pallas_call(functools.partial(kernel, n), out_shape=(jax.ShapeDtypeStr...  27.7 us
    pallas_call x1, Pallas kernels, on_device(): pl.pallas_call(unravel, out_shape=(jax.ShapeDtypeStruct((seasons, rows, c...  1.94 us

profile of v2, /device:TPU:1, one launch (start us, length us, event | category | flops | bytes accessed | tf_op | source)
XLA Modules:
  0.0 30.3 jit_solution(5519625546080470768)
XLA Ops:
  0.6 27.7 %shard_map.113 = (f32[10,128,128]{2,1,0:T(8,128)}, f32[128,128]{1,0:T(8,128)}) custom-call(f32[8,16,1280]{2,1,0:T(8,128)} %noise_hbm.1, f32[31]{0:T(128)} %kern_row.1, f32[31]{0:T(128)} %kern_col.1, f32[256,1280]{1,0:T(8,128)} %bitcast.2, f32[16]{0:T(128)} %sens.1, s32[256,1280]{1,0:T(8,128)} %bitcast.3, f32[16,1280]{1,0:T(8,128)} %area_hbm.1, ...), custom_call_target="tpu_custom_call" | custom-call | tf_op jit(solution)/shard_map/pallas_call | solution.py:411
  28.3 1.9 %shard_map.114 = (f32[8,16,1280]{2,1,0:T(8,128)}, f32[8,16,102]{2,1,0:T(8,128)}) custom-call(f32[10,128,128]{2,1,0:T(8,128)} %get-tuple-element.4.pay, f32[128,128]{1,0:T(8,128)} %get-tuple-element.5.yields), custom_call_target="tpu_custom_call" | custom-call | tf_op jit(solution)/shard_map/pallas_call | solution.py:468
